TPU v7x, 256 devices: a whole 4x4x8 slice. The times are simulated.
256 devices in a mesh: prompt: 16 (over y, z_lo, core), resp: 16 (over z_hi, x).
Axes of the slice: x: 4, y: 4, z: 8 (z_hi: 4, z_lo: 2; z = z_hi * 2 + z_lo), core: 2. Of those that a mesh axis runs over, the one named last changes fastest.
Arguments:
- prefix_latent: bfloat16 [16, 256, 512], P('prompt', 'resp'), may hold values from -300 to 300
- prefix_rope: bfloat16 [16, 256, 64], P('prompt', 'resp'), may hold values from -600 to 600
- resp_latent: bfloat16 [16, 16, 80, 512], P('prompt', 'resp'), may hold values from -300 to 300
- resp_rope: bfloat16 [16, 16, 80, 64], P('prompt', 'resp'), may hold values from -6 to 6
- norm_gain: float32 [512], replicated, may hold values from 0.5 to 1.5
- queries: bfloat16 [16, 16, 80, 64, 576], P('prompt', 'resp'), may hold values from -6 to 6
- cotangent: bfloat16 [16, 16, 80, 64, 512], P('prompt', 'resp'), may hold values from -6 to 6
- lengths: int32 [16, 16], P('prompt', 'resp'), may hold values from 1 to 80, 800 in all within a row
- token_mask: int32 [16, 16, 80], P('prompt', 'resp'), may hold values 0 or 1
- rewards: float32 [16, 16], P('prompt', 'resp'), may hold values from -14 to 14
Outputs:
- grad_prefix_latent: float32 [16, 256, 512], P('prompt', 'resp')
- grad_prefix_rope: float32 [16, 256, 64], P('prompt', 'resp')
- grad_resp_latent: float32 [16, 16, 80, 512], P('prompt', 'resp')
- grad_resp_rope: float32 [16, 16, 80, 64], P('prompt', 'resp')
- grad_gain: float32 [512], replicated
All inputs are finite; a program needn't handle non-finite values. No bound on the sum of `lengths` or of `token_mask` on one device may be relied on, other than what follows from the above.
Results may differ from a plain program's by a relative error of at most 0.017.
Values may be sent and summed in bfloat16 or wider, within the bound.
A program may use at most 64 MiB of HBM per device.

v0:
```python
import jax
import jax.numpy as jnp
from jax import lax
from jax.sharding import PartitionSpec as P

SOFTMAX_SCALE = 192.0 ** (-0.5)
NORM_EPSILON = 1e-06


def normalize(raw_rows, gain_vector):
    values = raw_rows.astype(jnp.float32)
    inverse = lax.rsqrt(jnp.mean(values * values, axis=-1, keepdims=True) + NORM_EPSILON)
    normed = values * inverse
    return (normed, inverse, (normed * gain_vector).astype(jnp.bfloat16))


def norm_backward(upstream, normed, inverse, gain_vector):
    scaled = upstream * gain_vector
    expected = jnp.mean(scaled * normed, axis=-1, keepdims=True)
    gain_terms = jnp.sum(upstream * normed, axis=0)
    return ((scaled - normed * expected) * inverse, gain_terms)


def score_terms(query_block, grad_block, key_rows, lat_width):
    scores = (
        jnp.einsum("thd,kd->htk", query_block, key_rows, preferred_element_type=jnp.float32)
        * SOFTMAX_SCALE
    )
    grad_soft = jnp.einsum(
        "the,ke->htk", grad_block, key_rows[:, :lat_width], preferred_element_type=jnp.float32
    )
    return (scores, grad_soft)


def finish(query_block, grad_block, prefix_part, local_part):
    maximum = jnp.maximum(
        jnp.max(prefix_part[0], axis=-1, keepdims=True),
        jnp.max(local_part[0], axis=-1, keepdims=True),
    )
    exp_prefix = jnp.exp(prefix_part[0] - maximum)
    exp_local = jnp.exp(local_part[0] - maximum)
    denominator = jnp.sum(exp_prefix, axis=-1, keepdims=True) + jnp.sum(
        exp_local, axis=-1, keepdims=True
    )
    soft_prefix = exp_prefix / denominator
    soft_local = exp_local / denominator
    expected = jnp.sum(soft_prefix * prefix_part[1], axis=-1, keepdims=True) + jnp.sum(
        soft_local * local_part[1], axis=-1, keepdims=True
    )
    results = []
    for softmax_rows, grad_soft in ((soft_prefix, prefix_part[1]), (soft_local, local_part[1])):
        grad_scores = (softmax_rows * (grad_soft - expected) * SOFTMAX_SCALE).astype(jnp.bfloat16)
        key_grads = jnp.einsum(
            "htk,thd->kd", grad_scores, query_block, preferred_element_type=jnp.float32
        )
        value_grads = jnp.einsum(
            "htk,the->ke",
            softmax_rows.astype(jnp.bfloat16),
            grad_block,
            preferred_element_type=jnp.float32,
        )
        results.append((key_grads, value_grads))
    return (results[0], results[1])


def per_device(
    prefix_latent,
    prefix_rope,
    resp_latent,
    resp_rope,
    norm_gain,
    queries,
    cotangent,
    lengths,
    token_mask,
    rewards,
):
    resp_count = lax.axis_size("resp")
    reward_sum = lax.psum(rewards[0, 0], "resp")
    advantage = rewards[0, 0] - reward_sum / resp_count
    query_rows = queries[0, 0]
    upstream_rows = cotangent[0, 0]
    row_count = query_rows.shape[0]
    head_count = query_rows.shape[1]
    lat_width = upstream_rows.shape[-1]
    head_block = 8
    block_count = head_count // head_block
    positions = jnp.arange(row_count)
    live_rows = (positions < lengths[0, 0]) & (token_mask[0, 0] > 0)
    weights = jnp.where(live_rows, -advantage, 0.0)
    grad_out = (weights[:, None, None] * upstream_rows).astype(jnp.bfloat16)
    causal = positions[None, :] <= positions[:, None]
    pre_normed, pre_inverse, pre_lat = normalize(prefix_latent[0], norm_gain)
    res_normed, res_inverse, res_lat = normalize(resp_latent[0, 0], norm_gain)
    local_keys = jnp.concatenate([res_lat, resp_rope[0, 0]], axis=1)
    gathered_lat, gathered_rope = (
        lax.all_gather(pre_lat, "resp", axis=0, tiled=True),
        lax.all_gather(prefix_rope[0], "resp", axis=0, tiled=True),
    )
    prefix_keys = jnp.concatenate([gathered_lat, gathered_rope], axis=1)
    prefix_count = prefix_keys.shape[0]
    key_width = prefix_keys.shape[1]

    def slices(block_index):
        start = block_index * head_block
        return (
            lax.dynamic_slice_in_dim(query_rows, start, head_block, 1),
            lax.dynamic_slice_in_dim(grad_out, start, head_block, 1),
        )

    def local_terms(query_block, grad_block):
        scores, grad_soft = score_terms(query_block, grad_block, local_keys, lat_width)
        return (jnp.where(causal, scores, -jnp.inf), grad_soft)

    def accumulate(carried, query_block, grad_block, local_part):
        prefix_part = score_terms(query_block, grad_block, prefix_keys, lat_width)
        (prefix_key, prefix_value), (local_key, local_value) = finish(
            query_block, grad_block, prefix_part, local_part
        )
        return (
            carried[0] + prefix_key,
            carried[1] + prefix_value,
            carried[2] + local_key,
            carried[3] + local_value,
        )

    start_carry = (
        jnp.zeros((prefix_count, key_width), jnp.float32),
        jnp.zeros((prefix_count, lat_width), jnp.float32),
        jnp.zeros((row_count, key_width), jnp.float32),
        jnp.zeros((row_count, lat_width), jnp.float32),
    )

    def joint_step(carried, block_index):
        query_block, grad_block = slices(block_index)
        return (
            accumulate(carried, query_block, grad_block, local_terms(query_block, grad_block)),
            None,
        )

    carried, unused_out = lax.scan(joint_step, start_carry, jnp.arange(block_count))
    prefix_key_grads, prefix_value_grads, local_key_grads, local_value_grads = carried
    prefix_latent_grad = prefix_key_grads[:, :lat_width] + prefix_value_grads
    prefix_rope_grad = prefix_key_grads[:, lat_width:]
    whole_latent, whole_rope = lax.psum((prefix_latent_grad, prefix_rope_grad), "resp")
    shard_rows = prefix_latent.shape[1]
    offset = lax.axis_index("resp") * shard_rows
    own_latent = lax.dynamic_slice_in_dim(whole_latent, offset, shard_rows, 0)
    own_rope = lax.dynamic_slice_in_dim(whole_rope, offset, shard_rows, 0)
    grad_prefix_latent, gain_prefix = norm_backward(own_latent, pre_normed, pre_inverse, norm_gain)
    local_latent = local_key_grads[:, :lat_width] + local_value_grads
    grad_resp_latent, gain_local = norm_backward(local_latent, res_normed, res_inverse, norm_gain)
    grad_gain = lax.psum(gain_prefix + gain_local, ("prompt", "resp"))
    return (
        grad_prefix_latent[None],
        own_rope[None],
        grad_resp_latent[None, None],
        local_key_grads[:, lat_width:][None, None],
        grad_gain,
    )


def solution(mesh):
    placed = (
        P("prompt", "resp", None),
        P("prompt", "resp", None),
        P("prompt", "resp", None, None),
        P("prompt", "resp", None, None),
        P(),
        P("prompt", "resp", None, None, None),
        P("prompt", "resp", None, None, None),
        P("prompt", "resp"),
        P("prompt", "resp", None),
        P("prompt", "resp"),
    )
    return jax.shard_map(
        per_device,
        mesh=mesh,
        in_specs=placed,
        out_specs=(
            P("prompt", "resp", None),
            P("prompt", "resp", None),
            P("prompt", "resp", None, None),
            P("prompt", "resp", None, None),
            P(),
        ),
        check_vma=False,
    )
```

profile of v0, /device:TPU:1, one launch (start us, length us, event | category | flops | bytes accessed | tf_op | source)
XLA Modules:
  0.0 510.3 jit_solution(2613937703221345436)
XLA Ops:
  8.9 41.9 %all_gather.6 = bf16[256,512]{1,0:T(8,128)(2,1)S(1)} all-gather(bf16[16,512]{1,0:T(8,128)(2,1)S(1)} %fusion.51), channel_id=1, replica_groups=mesh['prompt'=16,'resp'=16] {'resp'}, dimensions={0}, use_global_device_ids=true | all-gather | bytes 278528 | tf_op jit(solution)/shard_map/all_gather | solution.py:97
  50.8 32.0 %all-gather = bf16[1,256,64]{2,1,0:T(8,128)(2,1)S(1)} all-gather(bf16[1,16,64]{2,1,0:T(8,128)(2,1)} %param.13), channel_id=2, replica_groups=mesh['prompt'=16,'resp'=16] {'resp'}, dimensions={1}, use_global_device_ids=true | all-gather | bytes 34816 | tf_op jit(solution)/shard_map/all_gather | solution.py:98
  86.6 34.0 %psum.28 = f32[]{:T(128)} all-reduce(f32[]{:T(128)} %bitcast.9), channel_id=1, replica_groups=mesh['prompt'=16,'resp'=16] {'resp'}, use_global_device_ids=true, to_apply=%region_0.0 | all-reduce | flops 1 | bytes 8 | tf_op jit(solution)/shard_map/psum | solution.py:79
  122.5 6.9 %fusion.35 = bf16[80,64,512]{2,1,0:T(8,128)(2,1)} fusion(bf16[1,1,80,64,512]{4,3,2,1,0:T(8,128)(2,1)} %param.18, f32[80]{0:T(128)S(1)} %fusion.58), kind=kLoop, calls=%fused_computation.48 | loop fusion | flops 7864320 | bytes 10486080 | tf_op jit(solution)/shard_map/convert_element_type | solution.py:91
  129.5 110.8 %while.17 = (s32[]{:T(128)}, f32[256,576]{0,1:T(8,128)S(1)}, f32[256,512]{1,0:T(8,128)}, f32[80,576]{1,0:T(8,128)S(1)}, f32[80,512]{1,0:T(8,128)}, /*index=5*/s3...) while((s32[]{:T(128)}, f32[256,576]{0,1:T(8,128)S(1)}, ...), condition=%wide.region_10.11_spmd.clone, body=%wide.region_3.10_spmd.clone.sunk | while | flops 940296576 | bytes 21213476 | solution.py:141
  130.7 1.2 constant_dynamic-slice_fusion.3
  133.5 2.4 fusion.97
  135.9 1.5 multiply_reduce_fusion.5
  137.4 1.6 multiply_reduce_fusion.4
  139.6 1.9 fusion.95
  144.6 1.2 constant_dynamic-slice_fusion.3
  147.3 2.4 fusion.97
  149.7 1.5 multiply_reduce_fusion.5
  151.2 1.6 multiply_reduce_fusion.4
  153.5 1.9 fusion.95
  158.4 1.2 constant_dynamic-slice_fusion.3
  161.2 2.4 fusion.97
  163.6 1.5 multiply_reduce_fusion.5
  165.1 1.6 multiply_reduce_fusion.4
  167.3 1.9 fusion.95
  172.3 1.2 constant_dynamic-slice_fusion.3
  175.0 2.4 fusion.97
  177.4 1.5 multiply_reduce_fusion.5
  178.9 1.6 multiply_reduce_fusion.4
  181.2 1.9 fusion.95
  186.1 1.2 constant_dynamic-slice_fusion.3
  188.9 2.4 fusion.97
  191.3 1.5 multiply_reduce_fusion.5
  192.8 1.6 multiply_reduce_fusion.4
  195.0 1.9 fusion.95
  202.7 2.4 fusion.97
  205.1 1.5 multiply_reduce_fusion.5
  206.6 1.6 multiply_reduce_fusion.4
  208.9 1.9 fusion.95
  216.6 2.4 fusion.97
  219.0 1.5 multiply_reduce_fusion.5
  220.5 1.6 multiply_reduce_fusion.4
  222.8 1.9 fusion.95
  227.7 1.2 constant_dynamic-slice_fusion.3
  230.4 2.4 fusion.97
  232.8 1.5 multiply_reduce_fusion.5
  234.4 1.6 multiply_reduce_fusion.4
  236.6 1.9 fusion.95
  241.1 1.9 slice_add_fusion
  245.0 1.7 fusion.44
  246.7 169.2 %all-reduce.3.cloned.1.call-done = (f32[256,512]{1,0:T(8,128)}, f32[256,64]{0,1:T(8,128)}) async-done(((f32[256,512]{1,0:T(8,128)}, f32[256,64]{0,1:T(8,128)}), (f32[256,512]{1,0:T(8,128)}, f32[256,64]{0,1:T(8,128)})) %all-reduce.3.cloned.1.call-update) | async-done | bytes 589840 | tf_op jit(solution)/shard_map/psum | solution.py:145
  416.8 83.7 %psum.31 = f32[512]{0:T(512)} all-reduce(f32[512]{0:T(512)S(1)} %add.81), channel_id=1, replica_groups=mesh['prompt'=16,'resp'=16] {'prompt','resp'}, use_global_device_ids=true, to_apply=%region_17.18 | all-reduce | flops 512 | bytes 4096 | tf_op jit(solution)/shard_map/psum | solution.py:153
  500.5 1.4 fusion.55
  (165 shorter events, 49.2 us)
Async XLA Ops:
  7.2 408.7 %all-reduce.3.cloned.1.call-start = ((), (), s32[]{:S(2)}) async-start(), calls=%async_computation | async-start | bytes 1179648 | tf_op jit(solution)/shard_map/psum | solution.py:145
  129.5 113.8 %copy-start = (bf16[1,1,80,512]{3,2,1,0:T(8,128)(2,1)S(1)}, bf16[1,1,80,512]{3,2,1,0:T(8,128)(2,1)}, u32[]{:S(2)}) copy-start(bf16[1,1,80,512]{3,2,1,0:T(8,128)(2,1)} %param.14) | copy-start | bytes 245764
  129.5 113.8 %copy-start.4 = (f32[512]{0:T(512)S(1)}, f32[512]{0:T(512)}, u32[]{:S(2)}) copy-start(f32[512]{0:T(512)} %param.16) | copy-start | bytes 6148
  129.5 286.4 %copy-start.3 = (bf16[1,16,512]{2,1,0:T(8,128)(2,1)S(1)}, bf16[1,16,512]{2,1,0:T(8,128)(2,1)}, u32[]{:S(2)}) copy-start(bf16[1,16,512]{2,1,0:T(8,128)(2,1)} %param.12) | copy-start | bytes 49156
  133.5 6.1 %copy-start.1 = (f32[256,512]{1,0:T(8,128)S(1)}, f32[256,512]{1,0:T(8,128)}, u32[]{:S(2)}) copy-start(f32[256,512]{1,0:T(8,128)} %get-tuple-element.277) | copy-start | bytes 1572868 | tf_op jit(solution)/shard_map/while
  141.5 0.8 copy-start.2
  147.3 6.2 %copy-start.1 = (f32[256,512]{1,0:T(8,128)S(1)}, f32[256,512]{1,0:T(8,128)}, u32[]{:S(2)}) copy-start(f32[256,512]{1,0:T(8,128)} %get-tuple-element.277) | copy-start | bytes 1572868 | tf_op jit(solution)/shard_map/while
  155.4 0.8 copy-start.2
  161.2 6.2 %copy-start.1 = (f32[256,512]{1,0:T(8,128)S(1)}, f32[256,512]{1,0:T(8,128)}, u32[]{:S(2)}) copy-start(f32[256,512]{1,0:T(8,128)} %get-tuple-element.277) | copy-start | bytes 1572868 | tf_op jit(solution)/shard_map/while
  169.2 0.8 copy-start.2
  175.0 6.2 %copy-start.1 = (f32[256,512]{1,0:T(8,128)S(1)}, f32[256,512]{1,0:T(8,128)}, u32[]{:S(2)}) copy-start(f32[256,512]{1,0:T(8,128)} %get-tuple-element.277) | copy-start | bytes 1572868 | tf_op jit(solution)/shard_map/while
  183.1 0.8 copy-start.2
  188.9 6.2 %copy-start.1 = (f32[256,512]{1,0:T(8,128)S(1)}, f32[256,512]{1,0:T(8,128)}, u32[]{:S(2)}) copy-start(f32[256,512]{1,0:T(8,128)} %get-tuple-element.277) | copy-start | bytes 1572868 | tf_op jit(solution)/shard_map/while
  196.9 0.8 copy-start.2
  202.7 6.2 %copy-start.1 = (f32[256,512]{1,0:T(8,128)S(1)}, f32[256,512]{1,0:T(8,128)}, u32[]{:S(2)}) copy-start(f32[256,512]{1,0:T(8,128)} %get-tuple-element.277) | copy-start | bytes 1572868 | tf_op jit(solution)/shard_map/while
  210.8 0.8 copy-start.2
  216.6 6.2 %copy-start.1 = (f32[256,512]{1,0:T(8,128)S(1)}, f32[256,512]{1,0:T(8,128)}, u32[]{:S(2)}) copy-start(f32[256,512]{1,0:T(8,128)} %get-tuple-element.277) | copy-start | bytes 1572868 | tf_op jit(solution)/shard_map/while
  224.6 0.8 copy-start.2
  230.4 6.2 %copy-start.1 = (f32[256,512]{1,0:T(8,128)S(1)}, f32[256,512]{1,0:T(8,128)}, u32[]{:S(2)}) copy-start(f32[256,512]{1,0:T(8,128)} %get-tuple-element.277) | copy-start | bytes 1572868 | tf_op jit(solution)/shard_map/while
  238.5 0.8 copy-start.2
Sparse Core Ops, SparseCore 0:
  243.2 172.6 all-reduce.2
where the time goes:
time: 513 us; the launch traced here: 510 us
  blocking collectives  192 us (37%)
  waiting for transfers between devices  169 us (33%)
  matrix products  76.4 us (15%)
  other arithmetic  25.5 us (5%)
  local copies, waits for them, and re-layouts  25 us (5%)
  between operations  16.1 us (3%)
  loops' own time  6.4 us (1%)
    psum x1, waiting for transfers between devices, per_device(): lax.psum((prefix_latent_grad, prefix_rope_grad), 'resp')  169 us
    psum x1, blocking collectives, per_device(): grad_gain = lax.psum(gain_prefix + gain_local, ('prompt', 'resp'))  83.7 us
    all_gather x1, blocking collectives, per_device(): lax.all_gather(pre_lat, 'resp', axis=0, tiled=True)  41.9 us
    psum x1, blocking collectives, per_device(): reward_sum = lax.psum(rewards[0, 0], 'resp')  34 us
    dot_general x16, matrix products, finish(): jnp.einsum('htk,the->ke', softmax_rows.astype(jnp.bfloat16), grad_block,...  34 us
    all_gather x1, blocking collectives, per_device(): lax.all_gather(prefix_rope[0], 'resp', axis=0, tiled=True)  32 us
    dot_general x16, matrix products, score_terms(): jnp.einsum('the,ke->htk', grad_block, key_rows[:, :lat_width], preferred_...  24.6 us
    dot_general x16, matrix products, finish(): jnp.einsum('htk,thd->kd', grad_scores, query_block, preferred_element_typ...  10.4 us
  transfers between devices with their start and end apart: 1, of which 1 were waited for; matrix products, arithmetic and copies ran while one was open for 1% of the time, Pallas kernels for 0%

commit v1 on v0

v1 whole, which is shorter than its diff:
```python
import functools

import jax
import jax.numpy as jnp
from jax import lax
from jax.experimental import pallas as pl
from jax.experimental.pallas import tpu as pltpu
from jax.sharding import PartitionSpec as P

SOFTMAX_SCALE = 192.0 ** (-0.5)
LOG2E = 1.4426950408889634
NORM_EPSILON = 1e-06
NT = (((1,), (1,)), ((), ()))
LINE = 4
BLK = 512
MESH = pl.DeviceIdType.MESH
F32, BF16 = jnp.float32, jnp.bfloat16


def normed_rows(raw):
    values = raw.astype(F32)
    inverse = lax.rsqrt(jnp.mean(values * values, axis=-1, keepdims=True) + NORM_EPSILON)
    return values * inverse, inverse


def norm_backward(upstream, normed, inverse, gain):
    scaled = upstream * gain
    expected = jnp.mean(scaled * normed, axis=-1, keepdims=True)
    return (scaled - normed * expected) * inverse


def kernel(
    prompts,
    pl_hbm, pr_hbm, rl_hbm, rr_hbm, gain_hbm, q_hbm, c_hbm, len_hbm, mask_hbm, rew_hbm,
    o_pl, o_pr, o_rl, o_rr, o_gain,
    q_v, c_v, p_st, d_st, keys, normed, gathered, pl_v, pr_v, rl_v, rr_v, gain_v,
    len_s, mask_s, rew_s, acc, send_x, recv_x, send_z, recv_z, sum_z,
    gain_own, gain_x, gain_xs, gain_z, gain_zs, gain_p,
    load_sem, g_send, g_recv, x_send, x_recv, z_send, z_recv, gx_send, gx_recv,
    gz_send, gz_recv, gp_send, gp_recv,
):
    rows, lat = c_v.shape
    wide = q_v.shape[1]
    rope = wide - lat
    local = rl_v.shape[0]
    own = pl_v.shape[0]
    plen = own * LINE * LINE
    group = own * LINE

    me = lax.axis_index("resp")
    prompt = lax.axis_index("prompt")
    my_z, my_x = me // LINE, lax.rem(me, LINE)

    small = [
        pltpu.make_async_copy(src, dst, load_sem.at[i])
        for i, (src, dst) in enumerate(
            ((pl_hbm, pl_v), (pr_hbm, pr_v), (rew_hbm, rew_s), (rl_hbm, rl_v), (rr_hbm, rr_v),
             (gain_hbm, gain_v), (len_hbm, len_s), (mask_hbm, mask_s))
        )
    ]
    for copy in small:
        copy.start()

    def on_x(step):
        return lax.rem(my_x + step, LINE)

    def on_z(step):
        return lax.rem(my_z + step, LINE)

    barrier = pltpu.get_barrier_semaphore()
    for step in range(1, LINE):
        pl.semaphore_signal(barrier, inc=1, device_id={"resp": my_z * LINE + on_x(step)}, device_id_type=MESH)
        pl.semaphore_signal(barrier, inc=1, device_id={"resp": on_z(step) * LINE + my_x}, device_id_type=MESH)
    for step in range(1, prompts):
        pl.semaphore_signal(barrier, inc=1, device_id={"prompt": lax.rem(prompt + step, prompts)}, device_id_type=MESH)
    big = [
        pltpu.make_async_copy(q_hbm, q_v, load_sem.at[8]),
        pltpu.make_async_copy(c_hbm, c_v, load_sem.at[9]),
    ]
    for copy in big:
        copy.start()
    for copy in small[:3]:
        copy.wait()

    reward = jnp.full((own, rope), rew_s[0, 0], F32)
    high = reward.astype(BF16)
    rest = reward - high.astype(F32)
    mid = rest.astype(BF16)
    low = (rest - mid.astype(F32)).astype(BF16)
    lane = lax.broadcasted_iota(jnp.int32, (own, rope), 1)
    terms = jnp.where(
        lane == 0, high.astype(F32), jnp.where(lane == 1, mid.astype(F32), jnp.where(lane == 2, low.astype(F32), 0.0))
    )
    mine = gathered.at[my_x, my_z]
    mine[:, :lat] = pl_v[...]
    mine[:, lat:] = jnp.concatenate([pr_v[...].astype(F32), terms], axis=1).astype(BF16)

    pl.semaphore_wait(barrier, 2 * (LINE - 1) + prompts - 1)
    along_z = []
    for step in range(1, LINE):
        copy = pltpu.make_async_remote_copy(
            src_ref=gathered.at[my_x, my_z], dst_ref=gathered.at[my_x, my_z],
            send_sem=g_send.at[step], recv_sem=g_recv.at[step],
            device_id={"resp": on_z(step) * LINE + my_x}, device_id_type=MESH,
        )
        copy.start()
        along_z.append(copy)

    for copy in small[3:]:
        copy.wait()
    gain = gain_v[...]
    res_normed, res_inverse = normed_rows(rl_v[...])
    normed[plen:, :] = res_normed
    keys[plen:, :lat] = (res_normed * gain).astype(BF16)
    eye = (
        lax.broadcasted_iota(jnp.int32, (local, local), 0) == lax.broadcasted_iota(jnp.int32, (local, local), 1)
    ).astype(F32).astype(BF16)
    keys[plen:, lat:] = lax.dot_general(eye, rr_v[...], NT, preferred_element_type=F32).astype(BF16)

    for copy in along_z:
        copy.wait()
    along_x = []
    for step in range(1, LINE):
        copy = pltpu.make_async_remote_copy(
            src_ref=gathered.at[my_x], dst_ref=gathered.at[my_x],
            send_sem=g_send.at[LINE + step], recv_sem=g_recv.at[LINE + step],
            device_id={"resp": my_z * LINE + on_x(step)}, device_id_type=MESH,
        )
        copy.start()
        along_x.append(copy)
    for copy in along_x:
        copy.wait()

    raw = gathered[...].reshape(plen, lat + 2 * rope)
    pre_normed, pre_inverse = normed_rows(raw[:, :lat])
    normed[:plen, :] = pre_normed
    keys[:plen, :lat] = (pre_normed * gain).astype(BF16)
    keys[:plen, lat:] = raw[:, lat : lat + rope]
    reward_sum = jnp.sum(raw[:, lat:].astype(F32)[:, rope:]) / own
    factor = reward_sum / (LINE * LINE) - rew_s[0, 0]

    for copy in big:
        copy.wait()
    heads = rows // local
    per_block = BLK // heads
    column = lax.broadcasted_iota(jnp.int32, (1, BLK), 1)
    key_at = lax.broadcasted_iota(jnp.int32, (local, BLK), 0)
    token_in = lax.broadcasted_iota(jnp.int32, (local, BLK), 1) // heads
    length = len_s[0, 0]

    def forward(block, carry):
        at = pl.ds(pl.multiple_of(block * BLK, BLK), BLK)
        first = block * per_block
        live = jnp.zeros((1, BLK), F32)
        for i in range(per_block):
            weight = jnp.where((first + i < length) & (mask_s[0, first + i] > 0), 1.0, 0.0)
            live = jnp.where((column >= i * heads) & (column < (i + 1) * heads), weight, live)
        scores = lax.dot_general(keys[...], q_v[at, :], NT, preferred_element_type=F32)
        grad_soft = lax.dot_general(keys[:, :lat], c_v[at, :], NT, preferred_element_type=F32)
        visible = key_at <= token_in + first
        scores = jnp.concatenate([scores[:plen], jnp.where(visible, scores[plen:], -jnp.inf)], axis=0)
        maximum = jnp.max(scores, axis=0, keepdims=True)
        powers = jnp.exp2((scores - maximum) * (SOFTMAX_SCALE * LOG2E))
        inverse = 1.0 / jnp.sum(powers, axis=0, keepdims=True)
        expected = jnp.sum(powers * grad_soft, axis=0, keepdims=True) * inverse
        soft = powers * (inverse * live)
        p_st[:, at] = soft.astype(BF16)
        d_st[:, at] = (soft * (grad_soft - expected)).astype(BF16)
        return carry

    lax.fori_loop(0, rows // BLK, forward, 0)

    def contract(stored, values, lo, hi):
        return jnp.dot(stored[...], values[:, lo:hi], preferred_element_type=F32)

    parts = ((0, 256), (256, 512), (512, 576))
    x_copies, gain_copies = [], []
    for part, (lo, hi) in enumerate(parts):
        total = contract(d_st, q_v, lo, hi) * SOFTMAX_SCALE
        if hi <= lat:
            total = total + contract(p_st, c_v, lo, hi)
        total = total * factor
        acc[:, lo:hi] = total
        send_x[:, :, lo:hi] = total[:plen].astype(BF16).reshape(LINE, group, hi - lo)
        started = []
        for step in range(1, LINE):
            copy = pltpu.make_async_remote_copy(
                src_ref=send_x.at[on_x(step), :, lo:hi], dst_ref=recv_x.at[step, :, lo:hi],
                send_sem=x_send.at[part, step], recv_sem=x_recv.at[part, step],
                device_id={"resp": my_z * LINE + on_x(step)}, device_id_type=MESH,
            )
            copy.start()
            started.append(copy)
        x_copies.append(started)
        if hi <= lat:
            gain_own[:, lo:hi] = jnp.sum(total * normed[:, lo:hi], axis=0, keepdims=True)

    for step in range(1, LINE):
        copy = pltpu.make_async_remote_copy(
            src_ref=gain_own, dst_ref=gain_x.at[step],
            send_sem=gx_send.at[step], recv_sem=gx_recv.at[step],
            device_id={"resp": my_z * LINE + on_x(step)}, device_id_type=MESH,
        )
        copy.start()
        gain_copies.append(copy)

    z_copies = []
    mine_rows = pl.ds(pl.multiple_of(my_x * group, group), group)
    for part, (lo, hi) in enumerate(parts):
        for copy in x_copies[part]:
            copy.wait()
        total = acc[mine_rows, lo:hi]
        for step in range(1, LINE):
            total = total + recv_x[step, :, lo:hi].astype(F32)
        sum_z[:, :, lo:hi] = total.reshape(LINE, own, hi - lo)
        send_z[:, :, lo:hi] = total.astype(BF16).reshape(LINE, own, hi - lo)
        started = []
        for step in range(1, LINE):
            copy = pltpu.make_async_remote_copy(
                src_ref=send_z.at[on_z(step), :, lo:hi], dst_ref=recv_z.at[step, :, lo:hi],
                send_sem=z_send.at[part, step], recv_sem=z_recv.at[part, step],
                device_id={"resp": on_z(step) * LINE + my_x}, device_id_type=MESH,
            )
            copy.start()
            started.append(copy)
        z_copies.append(started)

    for copy in gain_copies:
        copy.wait()
    total_gain = gain_own[...]
    for step in range(1, LINE):
        total_gain = total_gain + gain_x[step]
    gain_xs[...] = total_gain
    gain_copies = []
    for step in range(1, LINE):
        copy = pltpu.make_async_remote_copy(
            src_ref=gain_xs, dst_ref=gain_z.at[step],
            send_sem=gz_send.at[step], recv_sem=gz_recv.at[step],
            device_id={"resp": on_z(step) * LINE + my_x}, device_id_type=MESH,
        )
        copy.start()
        gain_copies.append(copy)

    o_rl[...] = norm_backward(acc[plen:, :lat], res_normed, res_inverse, gain)
    o_rr[...] = acc[plen:, lat:].T

    for copy in gain_copies:
        copy.wait()
    total_gain = gain_xs[...]
    for step in range(1, LINE):
        total_gain = total_gain + gain_z[step]
    gain_zs[...] = total_gain
    gain_copies = []
    for step in range(1, prompts):
        copy = pltpu.make_async_remote_copy(
            src_ref=gain_zs, dst_ref=gain_p.at[step],
            send_sem=gp_send.at[step], recv_sem=gp_recv.at[step],
            device_id={"prompt": lax.rem(prompt + step, prompts)}, device_id_type=MESH,
        )
        copy.start()
        gain_copies.append(copy)

    for started in z_copies:
        for copy in started:
            copy.wait()
    total = sum_z[my_z]
    for step in range(1, LINE):
        total = total + recv_z[step].astype(F32)
    own_normed, own_inverse = normed_rows(pl_v[...])
    o_pl[...] = norm_backward(total[:, :lat], own_normed, own_inverse, gain)
    o_pr[...] = total[:, lat:]

    for copy in gain_copies:
        copy.wait()
    total_gain = gain_zs[...]
    for step in range(1, prompts):
        total_gain = total_gain + gain_p[step]
    o_gain[...] = total_gain


def per_device(
    prompts, prefix_latent, prefix_rope, resp_latent, resp_rope, norm_gain, queries, cotangent, lengths, token_mask, rewards
):
    tokens, heads, wide = queries.shape[2:]
    lat = cotangent.shape[-1]
    rope = wide - lat
    own = prefix_latent.shape[1]
    rows = tokens * heads
    plen = own * LINE * LINE
    count = plen + tokens
    dma = pltpu.SemaphoreType.DMA
    out = pl.pallas_call(
        functools.partial(kernel, prompts),
        out_shape=(
            jax.ShapeDtypeStruct((own, lat), F32),
            jax.ShapeDtypeStruct((own, rope), F32),
            jax.ShapeDtypeStruct((tokens, lat), F32),
            jax.ShapeDtypeStruct((rope, tokens), F32),
            jax.ShapeDtypeStruct((1, lat), F32),
        ),
        in_specs=[pl.BlockSpec(memory_space=pl.ANY)] * 10,
        out_specs=[pl.BlockSpec(memory_space=pltpu.VMEM)] * 5,
        scratch_shapes=[
            pltpu.VMEM((rows, wide), BF16),
            pltpu.VMEM((rows, lat), BF16),
            pltpu.VMEM((count, rows), BF16),
            pltpu.VMEM((count, rows), BF16),
            pltpu.VMEM((count, wide), BF16),
            pltpu.VMEM((count, lat), F32),
            pltpu.VMEM((LINE, LINE, own, lat + 2 * rope), BF16),
            pltpu.VMEM((own, lat), BF16),
            pltpu.VMEM((own, rope), BF16),
            pltpu.VMEM((tokens, lat), BF16),
            pltpu.VMEM((rope, tokens), BF16),
            pltpu.VMEM((1, lat), F32),
            pltpu.SMEM((1, 1), jnp.int32),
            pltpu.SMEM((1, tokens), jnp.int32),
            pltpu.SMEM((1, 1), F32),
            pltpu.VMEM((count, wide), F32),
            pltpu.VMEM((LINE, own * LINE, wide), BF16),
            pltpu.VMEM((LINE, own * LINE, wide), BF16),
            pltpu.VMEM((LINE, own, wide), BF16),
            pltpu.VMEM((LINE, own, wide), BF16),
            pltpu.VMEM((LINE, own, wide), F32),
            pltpu.VMEM((1, lat), F32),
            pltpu.VMEM((LINE, 1, lat), F32),
            pltpu.VMEM((1, lat), F32),
            pltpu.VMEM((LINE, 1, lat), F32),
            pltpu.VMEM((1, lat), F32),
            pltpu.VMEM((prompts, 1, lat), F32),
            dma((10,)),
            dma((2 * LINE,)),
            dma((2 * LINE,)),
            dma((3, LINE)),
            dma((3, LINE)),
            dma((3, LINE)),
            dma((3, LINE)),
            dma((LINE,)),
            dma((LINE,)),
            dma((LINE,)),
            dma((LINE,)),
            dma((prompts,)),
            dma((prompts,)),
        ],
        compiler_params=pltpu.CompilerParams(
            collective_id=0, has_side_effects=True, vmem_limit_bytes=56 * 2**20
        ),
        name="grpo_backward",
    )(
        prefix_latent[0],
        prefix_rope[0],
        resp_latent[0, 0],
        resp_rope[0, 0].T,
        norm_gain[None],
        queries.reshape(rows, wide),
        cotangent.reshape(rows, lat),
        lengths,
        token_mask[0],
        rewards,
    )
    return (out[0][None], out[1][None], out[2][None, None], out[3].T[None, None], out[4][0])


def solution(mesh):
    placed = (
        P("prompt", "resp", None),
        P("prompt", "resp", None),
        P("prompt", "resp", None, None),
        P("prompt", "resp", None, None),
        P(),
        P("prompt", "resp", None, None, None),
        P("prompt", "resp", None, None, None),
        P("prompt", "resp"),
        P("prompt", "resp", None),
        P("prompt", "resp"),
    )
    return jax.shard_map(
        functools.partial(per_device, mesh.shape["prompt"]),
        mesh=mesh,
        in_specs=placed,
        out_specs=(
            P("prompt", "resp", None),
            P("prompt", "resp", None),
            P("prompt", "resp", None, None),
            P("prompt", "resp", None, None),
            P(),
        ),
        check_vma=False,
    )
```

time: 513 us -> 59.1 us (0.12)
  blocking collectives: 192 us -> 0 us
  waiting for transfers between devices: 169 us -> 0 us
  matrix products: 76.4 us -> 0 us
  Pallas kernels: 0 us -> 50 us
  other arithmetic: 25.5 us -> 0 us
  local copies, waits for them, and re-layouts: 25 us -> 6.88 us
  between operations: 16.1 us -> 1.94 us
  loops' own time: 6.4 us -> 0 us
    psum x1 -> x0, waiting for transfers between devices: 169 us -> none  [per_device(): lax.psum((prefix_latent_grad, prefix_rope_grad), 'resp')]
    psum x2 -> x0, blocking collectives: 118 us -> none  [the longest x1 83.7 us: per_device(): grad_gain = lax.psum(gain_prefix + gain_local, ('prompt', 'resp'))]
    dot_general x64 -> x0, matrix products: 76.4 us -> none  [the longest x16 34 us: finish(): jnp.einsum('htk,the->ke', softmax_rows.astype(jnp.bfloat16), grad_block,...]
    all_gather x2 -> x0, blocking collectives: 74 us -> none  [the longest x1 41.9 us: per_device(): lax.all_gather(pre_lat, 'resp', axis=0, tiled=True)]
    pallas_call x0 -> x1, Pallas kernels: none -> 50 us  [per_device(): pl.pallas_call(functools.partial(kernel, prompts), out_shape=(jax.ShapeDt...]
    dynamic_slice x18 -> x0, local copies, waits for them, and re-layouts: 16 us -> none  [the longest x8 9.76 us: slices(): lax.dynamic_slice_in_dim(query_rows, start, head_block, 1)]
    convert_element_type x11 -> x0, other arithmetic: 11.4 us -> none  [the longest x1 6.94 us: per_device(): grad_out = (weights[:, None, None] * upstream_rows).astype(jnp.bfloat16)]
    reduce_sum x20 -> x0, other arithmetic: 8.04 us -> none  [the longest x2 2.08 us: norm_backward(): gain_terms = jnp.sum(upstream * normed, axis=0)]
  transfers between devices with their start and end apart: 1 -> 0, of which waited for: 1 -> 0; matrix products, arithmetic and copies ran while one was open for 1% -> 0% of each run, Pallas kernels for 0% -> 0%
where the time goes in v1:
time: 59.1 us; the launch traced here: 58.8 us
  Pallas kernels  50 us (85%)
  local copies, waits for them, and re-layouts  6.88 us (12%)
  between operations  1.94 us (3%)
    pallas_call x1, Pallas kernels, per_device(): pl.pallas_call(functools.partial(kernel, prompts), out_shape=(jax.ShapeDt...  50 us
    unnamed x5, local copies, waits for them, and re-layouts  6.88 us

profile of v1, /device:TPU:1, one launch (start us, length us, event | category | flops | bytes accessed | tf_op | source)
XLA Modules:
  0.0 58.8 jit_solution(10376705660701075440)
XLA Ops:
  1.9 50.0 %grpo_backward.1 = (f32[16,512]{1,0:T(8,128)}, f32[16,64]{1,0:T(8,128)}, f32[80,512]{1,0:T(8,128)}, f32[64,80]{1,0:T(8,128)}, f32[1,512]{1,0:T(1,128)}) custom-call(bf16[16,512]{1,0:T(8,128)(2,1)} %bitcast.23, bf16[16,64]{1,0:T(8,128)(2,1)} %bitcast.26, bf16[80,512]{1,0:T(8,128)(2,1)} %bitcast.20, bf16[64,80]{1,0:T(8,128)(2,1)} %bitcast.24, ...), custom_call_target="tpu_custom_call" | custom-call | tf_op jit(solution)/shard_map/grpo_backward/pallas_call | solution.py:292
  51.9 1.4 %copy.22 = f32[1,16,512]{2,1,0:T(8,128)} copy(f32[1,16,512]{2,1,0:T(8,128)} %bitcast.22) | data formatting | bytes 65536
  53.3 1.3 %copy.23 = f32[1,16,64]{2,1,0:T(8,128)} copy(f32[1,16,64]{2,1,0:T(8,128)} %bitcast.25) | data formatting | bytes 8192
  54.6 1.6 %copy.24 = f32[1,1,80,512]{3,2,1,0:T(8,128)} copy(f32[1,1,80,512]{3,2,1,0:T(8,128)} %bitcast.19) | data formatting | bytes 327680
  56.2 1.4 %copy.25 = f32[1,1,80,64]{2,3,1,0:T(8,128)} copy(f32[1,1,80,64]{2,3,1,0:T(8,128)} %bitcast.21) | data formatting | bytes 40960
  57.5 1.2 %copy.26 = f32[512]{0:T(512)} copy(f32[512]{0:T(512)} %bitcast.28) | data formatting | bytes 4096

commit v2 on v1

v2 whole, which is shorter than its diff:
```python
import jax
import jax.numpy as jnp
from jax import lax
from jax.experimental import pallas as pl
from jax.experimental.pallas import tpu as pltpu
from jax.sharding import PartitionSpec as P

SOFTMAX_SCALE = 192.0 ** (-0.5)
LOG2E = 1.4426950408889634
NORM_EPSILON = 1e-06
NT = (((1,), (1,)), ((), ()))
LINE = 4
BLK = 512
UNROLL = 5
MESH = pl.DeviceIdType.MESH
F32, BF16 = jnp.float32, jnp.bfloat16


def normed_rows(raw):
    values = raw.astype(F32)
    inverse = lax.rsqrt(jnp.mean(values * values, axis=-1, keepdims=True) + NORM_EPSILON)
    return values * inverse, inverse


def norm_backward(upstream, normed, inverse, gain):
    scaled = upstream * gain
    expected = jnp.mean(scaled * normed, axis=-1, keepdims=True)
    return (scaled - normed * expected) * inverse


PEERS = LINE * LINE


def hops(offset):
    dz, dx = offset
    return 2 * min(dz, LINE - dz) + min(dx, LINE - dx)


OFFSETS = sorted(
    [(dz, dx) for dz in range(LINE) for dx in range(LINE)], key=lambda o: (o != (0, 0), o[0] > 0 and o[1] > 0, hops(o))
)
BACK = [OFFSETS.index(((LINE - dz) % LINE, (LINE - dx) % LINE)) for dz, dx in OFFSETS]
NEAR, FAR = (1, 7), (7, 16)
PARTS = ((0, 256), (256, 512), (512, 576))


def kernel(
    pl_hbm, pr_hbm, rl_hbm, rr_hbm, gain_hbm, q_hbm, c_hbm, len_hbm, mask_hbm, rew_hbm,
    o_pl, o_pr, o_rl, o_rr, o_gain,
    q_v, c_v, powers_v, grad_soft_v, stats, p_st, d_st, keys, normed, gathered, pl_v, pr_v, rl_v, rr_v, gain_v,
    len_s, mask_s, rew_s, acc, send_rows, recv_rows, gain_own, gain_a, gain_mid, gain_b,
    load_sem, g_send, g_recv, r_send, r_recv, a_send, a_recv, b_send, b_recv,
):
    rows, lat = c_v.shape
    wide = q_v.shape[1]
    rope = wide - lat
    local = rl_v.shape[0]
    own = pl_v.shape[0]
    count = keys.shape[0]

    me = lax.axis_index("resp")
    prompt = lax.axis_index("prompt")
    my_z, my_x = me // LINE, lax.rem(me, LINE)

    def shift(value, step):
        return lax.rem(value + step, LINE)

    def same_prompt(position):
        dz, dx = OFFSETS[position]
        return {"resp": shift(my_z, dz) * LINE + shift(my_x, dx)}

    def same_response(step):
        return {"prompt": lax.rem(prompt + step, PEERS)}

    small = [
        pltpu.make_async_copy(src, dst, load_sem.at[i])
        for i, (src, dst) in enumerate(
            ((pl_hbm, pl_v), (pr_hbm, pr_v), (rew_hbm, rew_s), (rl_hbm, rl_v), (rr_hbm, rr_v),
             (gain_hbm, gain_v), (len_hbm, len_s), (mask_hbm, mask_s))
        )
    ]
    for copy in small:
        copy.start()

    barrier = pltpu.get_barrier_semaphore()
    targets = [same_prompt(p) for p in range(NEAR[1] - 1, 0, -1)]
    targets += [same_response(s) for s in range(1, PEERS)]
    for target in targets:
        pl.semaphore_signal(barrier, inc=1, device_id=target, device_id_type=MESH)
    big = [
        pltpu.make_async_copy(q_hbm, q_v, load_sem.at[8]),
        pltpu.make_async_copy(c_hbm, c_v, load_sem.at[9]),
    ]
    for copy in big:
        copy.start()
    for copy in small:
        copy.wait()

    reward = jnp.full((own, rope), rew_s[0, 0], F32)
    high = reward.astype(BF16)
    rest = reward - high.astype(F32)
    mid = rest.astype(BF16)
    low = (rest - mid.astype(F32)).astype(BF16)
    lane = lax.broadcasted_iota(jnp.int32, (own, rope), 1)
    terms = jnp.where(
        lane == 0, high.astype(F32), jnp.where(lane == 1, mid.astype(F32), jnp.where(lane == 2, low.astype(F32), 0.0))
    )
    gathered[0, :, :lat] = pl_v[...]
    gathered[0, :, lat:] = jnp.concatenate([pr_v[...].astype(F32), terms], axis=1).astype(BF16)

    gain = gain_v[...]
    res_normed, res_inverse = normed_rows(rl_v[...])
    normed[:local, :] = res_normed
    keys[:local, :lat] = (res_normed * gain).astype(BF16)
    eye = (
        lax.broadcasted_iota(jnp.int32, (local, local), 0) == lax.broadcasted_iota(jnp.int32, (local, local), 1)
    ).astype(F32).astype(BF16)
    keys[:local, lat:] = lax.dot_general(eye, rr_v[...], NT, preferred_element_type=F32).astype(BF16)

    def place(first, last):
        lo, hi = local + first * own, local + last * own
        raw = gathered[first:last].reshape(hi - lo, lat + 2 * rope)
        rows_normed, rows_inverse = normed_rows(raw[:, :lat])
        normed[lo:hi, :] = rows_normed
        keys[lo:hi, :lat] = (rows_normed * gain).astype(BF16)
        keys[lo:hi, lat:] = raw[:, lat : lat + rope]
        return rows_normed, rows_inverse

    own_normed, own_inverse = place(0, 1)

    heads = rows // local
    per_block = BLK // heads
    column = lax.broadcasted_iota(jnp.int32, (1, BLK), 1)
    key_at = lax.broadcasted_iota(jnp.int32, (local, BLK), 0)
    token_in = lax.broadcasted_iota(jnp.int32, (local, BLK), 1) // heads
    length = len_s[0, 0]
    groups = tuple((local + a * own, local + b * own) for a, b in (NEAR, FAR))
    groups = ((0, groups[0][0]),) + groups

    def score(group):
        lo, hi = groups[group]

        def step(block, carry):
            at = pl.ds(pl.multiple_of(block * BLK, BLK), BLK)
            first = block * per_block
            scores = lax.dot_general(keys[lo:hi, :], q_v[at, :], NT, preferred_element_type=F32)
            grad_soft = lax.dot_general(keys[lo:hi, :lat], c_v[at, :], NT, preferred_element_type=F32)
            if group == 0:
                visible = key_at <= token_in + first
                scores = jnp.concatenate([jnp.where(visible, scores[:local], -jnp.inf), scores[local:]], axis=0)
            top = jnp.max(scores, axis=0, keepdims=True)
            powers = jnp.exp2((scores - top) * (SOFTMAX_SCALE * LOG2E))
            total = jnp.sum(powers, axis=0, keepdims=True)
            weighted = jnp.sum(powers * grad_soft, axis=0, keepdims=True)
            if group < 2:
                powers_v[lo:hi, at] = powers
                grad_soft_v[lo:hi, at] = grad_soft
                stats[3 * group : 3 * group + 1, at] = top
                stats[3 * group + 1 : 3 * group + 2, at] = total
                stats[3 * group + 2 : 3 * group + 3, at] = weighted
                return carry
            live = jnp.zeros((1, BLK), F32)
            for i in range(per_block):
                weight = jnp.where((first + i < length) & (mask_s[0, first + i] > 0), 1.0, 0.0)
                live = jnp.where((column >= i * heads) & (column < (i + 1) * heads), weight, live)
            tops = (stats[0:1, at], stats[3:4, at], top)
            maximum = jnp.maximum(jnp.maximum(tops[0], tops[1]), top)
            scales = [jnp.exp2((t - maximum) * (SOFTMAX_SCALE * LOG2E)) for t in tops]
            inverse = 1.0 / (scales[0] * stats[1:2, at] + scales[1] * stats[4:5, at] + scales[2] * total)
            expected = (scales[0] * stats[2:3, at] + scales[1] * stats[5:6, at] + scales[2] * weighted) * inverse
            for g, (a, b) in enumerate(groups):
                part = powers if g == 2 else powers_v[a:b, at]
                grads = grad_soft if g == 2 else grad_soft_v[a:b, at]
                soft = part * (scales[g] * inverse * live)
                p_st[a:b, at] = soft.astype(BF16)
                d_st[a:b, at] = (soft * (grads - expected)).astype(BF16)
            return carry

        lax.fori_loop(0, rows // BLK, step, 0, unroll=UNROLL)

    for copy in big:
        copy.wait()
    score(0)

    pl.semaphore_wait(barrier, len(targets))
    gathers = {}

    def pass_on(block, offset):
        (dz, dx), (ez, ex) = OFFSETS[block], offset
        there = OFFSETS.index(((dz - ez) % LINE, (dx - ex) % LINE))
        copy = pltpu.make_async_remote_copy(
            src_ref=gathered.at[block], dst_ref=gathered.at[there],
            send_sem=g_send.at[there], recv_sem=g_recv.at[there],
            device_id=same_prompt(OFFSETS.index(offset)), device_id_type=MESH,
        )
        copy.start()
        gathers[there] = copy

    for dz in (2, 1, 3):
        pass_on(0, (dz, 0))
    for dx in (2, 1, 3):
        pass_on(0, (0, dx))
    for dz in (1, 3, 2):
        block = OFFSETS.index((dz, 0))
        gathers[block].wait_recv()
        for dx in (2, 1, 3):
            pass_on(block, (0, dx))
    for dx in (1, 3, 2):
        gathers[OFFSETS.index((0, dx))].wait_recv()
    place(*NEAR)
    score(1)
    for p in range(*FAR):
        gathers[p].wait_recv()
    place(*FAR)
    score(2)
    for p in range(1, PEERS):
        gathers[p].wait_send()
    reward_sum = jnp.sum(gathered[:, :, lat:].astype(F32).reshape(PEERS * own, 2 * rope)[:, rope:]) / own
    factor = reward_sum / PEERS - rew_s[0, 0]

    def contract(stored, values, lo, hi):
        return jnp.dot(stored[...], values[:, lo:hi], preferred_element_type=F32)

    reduces = []
    for part, (lo, hi) in enumerate(PARTS):
        total = contract(d_st, q_v, lo, hi)
        if hi <= lat:
            total = total + contract(p_st, c_v, lo, hi) * (1.0 / SOFTMAX_SCALE)
        total = total * factor
        acc[:, lo:hi] = total
        if hi <= lat:
            gain_own[:, lo:hi] = jnp.sum(total * normed[:, lo:hi], axis=0, keepdims=True)
        if hi == lat:
            near = []
            for step in range(1, PEERS):
                copy = pltpu.make_async_remote_copy(
                    src_ref=gain_own, dst_ref=gain_a.at[BACK[step]],
                    send_sem=a_send.at[step], recv_sem=a_recv.at[BACK[step]],
                    device_id=same_prompt(step), device_id_type=MESH,
                )
                copy.start()
                near.append(copy)
        send_rows[:, :, lo:hi] = total[local:].astype(BF16).reshape(PEERS, own, hi - lo)
        for p in range(PEERS - 1, 0, -1):
            copy = pltpu.make_async_remote_copy(
                src_ref=send_rows.at[p, :, lo:hi], dst_ref=recv_rows.at[BACK[p], :, lo:hi],
                send_sem=r_send.at[part, p], recv_sem=r_recv.at[part, BACK[p]],
                device_id=same_prompt(p), device_id_type=MESH,
            )
            copy.start()
            reduces.append(copy)

    for copy in near:
        copy.wait()
    total_gain = gain_own[...]
    for step in range(1, PEERS):
        total_gain = total_gain + gain_a[step]
    gain_mid[...] = total_gain
    far = []
    for step in range(1, PEERS):
        copy = pltpu.make_async_remote_copy(
            src_ref=gain_mid, dst_ref=gain_b.at[step],
            send_sem=b_send.at[step], recv_sem=b_recv.at[step],
            device_id=same_response(step), device_id_type=MESH,
        )
        copy.start()
        far.append(copy)

    o_rl[...] = norm_backward(acc[:local, :lat], res_normed, res_inverse, gain)
    o_rr[...] = acc[:local, lat:].T
    for copy in reduces:
        copy.wait()
    total = acc[local : local + own, :]
    for p in range(1, PEERS):
        total = total + recv_rows[p].astype(F32)
    o_pl[...] = norm_backward(total[:, :lat], own_normed, own_inverse, gain)
    o_pr[...] = total[:, lat:]

    for copy in far:
        copy.wait()
    total_gain = gain_mid[...]
    for step in range(1, PEERS):
        total_gain = total_gain + gain_b[step]
    o_gain[...] = total_gain


def per_device(
    prefix_latent, prefix_rope, resp_latent, resp_rope, norm_gain, queries, cotangent, lengths, token_mask, rewards
):
    tokens, heads, wide = queries.shape[2:]
    lat = cotangent.shape[-1]
    rope = wide - lat
    own = prefix_latent.shape[1]
    rows = tokens * heads
    count = own * PEERS + tokens
    vmem, dma = pltpu.VMEM, pltpu.SemaphoreType.DMA
    shapes = ((own, lat), (own, rope), (tokens, lat), (rope, tokens), (1, lat))
    out = pl.pallas_call(
        kernel,
        out_shape=tuple(pltpu.VMEM(s, F32) for s in shapes),
        in_specs=[pl.BlockSpec(memory_space=pl.ANY)] * 10,
        out_specs=[pl.BlockSpec(memory_space=pltpu.VMEM)] * 5,
        scratch_shapes=[
            vmem((rows, wide), BF16),
            vmem((rows, lat), BF16),
            vmem((tokens + own * NEAR[1], rows), F32),
            vmem((tokens + own * NEAR[1], rows), F32),
            vmem((8, rows), F32),
            vmem((count, rows), BF16),
            vmem((count, rows), BF16),
            vmem((count, wide), BF16),
            vmem((count, lat), F32),
            vmem((PEERS, own, lat + 2 * rope), BF16),
            vmem((own, lat), BF16),
            vmem((own, rope), BF16),
            vmem((tokens, lat), BF16),
            vmem((rope, tokens), BF16),
            vmem((1, lat), F32),
            pltpu.SMEM((1, 1), jnp.int32),
            pltpu.SMEM((1, tokens), jnp.int32),
            pltpu.SMEM((1, 1), F32),
            vmem((count, wide), F32),
            vmem((PEERS, own, wide), BF16),
            vmem((PEERS, own, wide), BF16),
            vmem((1, lat), F32),
            vmem((PEERS, 1, lat), F32),
            vmem((1, lat), F32),
            vmem((PEERS, 1, lat), F32),
            dma((10,)),
            dma((PEERS,)),
            dma((PEERS,)),
            dma((len(PARTS), PEERS)),
            dma((len(PARTS), PEERS)),
            dma((PEERS,)),
            dma((PEERS,)),
            dma((PEERS,)),
            dma((PEERS,)),
        ],
        compiler_params=pltpu.CompilerParams(
            collective_id=0, has_side_effects=True, vmem_limit_bytes=56 * 2**20
        ),
        name="grpo_backward",
    )(
        prefix_latent[0],
        prefix_rope[0],
        resp_latent[0, 0],
        resp_rope[0, 0].T,
        norm_gain[None],
        queries.reshape(rows, wide),
        cotangent.reshape(rows, lat),
        lengths,
        token_mask[0],
        rewards,
    )
    out = [value * SOFTMAX_SCALE for value in out]
    return (out[0][None], out[1][None], out[2][None, None], out[3].T[None, None], out[4][0])


def solution(mesh):
    placed = (
        P("prompt", "resp", None),
        P("prompt", "resp", None),
        P("prompt", "resp", None, None),
        P("prompt", "resp", None, None),
        P(),
        P("prompt", "resp", None, None, None),
        P("prompt", "resp", None, None, None),
        P("prompt", "resp"),
        P("prompt", "resp", None),
        P("prompt", "resp"),
    )
    return jax.shard_map(
        per_device,
        mesh=mesh,
        in_specs=placed,
        out_specs=(
            P("prompt", "resp", None),
            P("prompt", "resp", None),
            P("prompt", "resp", None, None),
            P("prompt", "resp", None, None),
            P(),
        ),
        check_vma=False,
    )
```

time: 59.1 us -> 52.9 us (0.90)
  local copies, waits for them, and re-layouts: 6.88 us -> 0 us
  other arithmetic: 0 us -> 3.1 us
  Pallas kernels: 50 us -> 47.7 us
    unnamed x5 -> x0, local copies, waits for them, and re-layouts: 6.88 us -> none
    broadcast_in_dim x0 -> x4, other arithmetic: none -> 2.52 us  [the longest x1 0.68 us: per_device(): out[2][None, None]]
    pallas_call x1, Pallas kernels: 50 us -> 47.7 us  [per_device(): pl.pallas_call(kernel, out_shape=tuple((pltpu.VMEM(s, F32) for s in shape...]
where the time goes in v2:
time: 52.9 us; the launch traced here: 52.7 us
  Pallas kernels  47.7 us (90%)
  other arithmetic  3.1 us (6%)
  between operations  1.94 us (4%)
    pallas_call x1, Pallas kernels, per_device(): pl.pallas_call(kernel, out_shape=tuple((pltpu.VMEM(s, F32) for s in shape...  47.7 us

profile of v2, /device:TPU:1, one launch (start us, length us, event | category | flops | bytes accessed | tf_op | source)
XLA Modules:
  0.0 52.7 jit_solution(5881278943366127159)
XLA Ops:
  1.9 47.7 %grpo_backward.1 = (f32[16,512]{1,0:T(8,128)S(1)}, f32[16,64]{1,0:T(8,128)S(1)}, f32[80,512]{1,0:T(8,128)S(1)}, f32[64,80]{1,0:T(8,128)S(1)}, f32[1,512]{1,0:T(1,128)S(1)}) custom-call(bf16[16,512]{1,0:T(8,128)(2,1)} %bitcast.24, bf16[16,64]{1,0:T(8,128)(2,1)} %bitcast.26, bf16[80,512]{1,0:T(8,128)(2,1)} %bitcast.23, bf16[64,80]{1,0:T(8,128)(2,1)} %bitcast.25, ...), custom_call_target="tpu_custom_call" | custom-call | tf_op jit(solution)/shard_map/grpo_backward/pallas_call | solution.py:298
  49.6 0.6 %multiply_bitcast_fusion.2 = f32[1,16,512]{2,1,0:T(8,128)} fusion(f32[16,512]{1,0:T(8,128)S(1)} %get-tuple-element.10), kind=kLoop, calls=%fused_computation.2 | loop fusion | flops 8192 | bytes 65536 | tf_op jit(solution)/shard_map/broadcast_in_dim | solution.py:356
  50.3 0.6 %broadcast_multiply_fusion = f32[1,512]{1,0:T(1,128)} fusion(f32[1,512]{1,0:T(1,128)S(1)} %get-tuple-element.14), kind=kLoop, calls=%fused_computation.4 | loop fusion | flops 512 | bytes 4096 | tf_op jit(solution)/shard_map/mul | solution.py:355
  50.8 0.6 %multiply_bitcast_fusion.3 = f32[1,16,64]{2,1,0:T(8,128)} fusion(f32[16,64]{1,0:T(8,128)S(1)} %get-tuple-element.11), kind=kLoop, calls=%fused_computation.3 | loop fusion | flops 1024 | bytes 8192 | tf_op jit(solution)/shard_map/broadcast_in_dim | solution.py:356
  51.4 0.6 %multiply_bitcast_fusion.1 = f32[1,1,80,64]{2,3,1,0:T(8,128)} fusion(f32[64,80]{1,0:T(8,128)S(1)} %get-tuple-element.13), kind=kLoop, calls=%fused_computation.1 | loop fusion | flops 5120 | bytes 40960 | tf_op jit(solution)/shard_map/broadcast_in_dim | solution.py:356
  52.1 0.7 %multiply_bitcast_fusion = f32[1,1,80,512]{3,2,1,0:T(8,128)} fusion(f32[80,512]{1,0:T(8,128)S(1)} %get-tuple-element.12), kind=kLoop, calls=%fused_computation | loop fusion | flops 40960 | bytes 327680 | tf_op jit(solution)/shard_map/broadcast_in_dim | solution.py:356

commit v3 on v2

--- a/solution.py
+++ b/solution.py
@@ -48,8 +48,8 @@
     pl_hbm, pr_hbm, rl_hbm, rr_hbm, gain_hbm, q_hbm, c_hbm, len_hbm, mask_hbm, rew_hbm,
     o_pl, o_pr, o_rl, o_rr, o_gain,
     q_v, c_v, powers_v, grad_soft_v, stats, p_st, d_st, keys, normed, gathered, pl_v, pr_v, rl_v, rr_v, gain_v,
-    len_s, mask_s, rew_s, acc, send_rows, recv_rows, gain_own, gain_a, gain_mid, gain_b,
-    load_sem, g_send, g_recv, r_send, r_recv, a_send, a_recv, b_send, b_recv,
+    len_s, mask_s, rew_s, acc, send_x, recv_x, send_z, recv_z, gain_own, gain_a, gain_mid, gain_b,
+    token, load_sem, g_send, g_recv, x_send, x_recv, z_send, z_recv, a_send, a_recv, b_send, b_recv,
 ):
     rows, lat = c_v.shape
     wide = q_v.shape[1]
@@ -71,6 +71,12 @@
 
     def same_response(step):
         return {"prompt": lax.rem(prompt + step, PEERS)}
+
+    my_y, my_low, my_core = prompt // LINE, lax.rem(prompt, LINE) // 2, lax.rem(prompt, 2)
+
+    def near_prompt(dy, dlow, dcore):
+        low, core = lax.rem(my_low + dlow, 2), lax.rem(my_core + dcore, 2)
+        return {"prompt": shift(my_y, dy) * LINE + low * 2 + core}
 
     small = [
         pltpu.make_async_copy(src, dst, load_sem.at[i])
@@ -83,13 +89,18 @@
         copy.start()
 
     barrier = pltpu.get_barrier_semaphore()
-    targets = [same_prompt(p) for p in range(NEAR[1] - 1, 0, -1)]
-    targets += [same_response(s) for s in range(1, PEERS)]
+    targets = [same_prompt(OFFSETS.index(o)) for o in ((1, 0), (3, 0), (0, 2), (0, 1), (0, 3))]
+    targets += [
+        near_prompt(dy, dlow, dcore)
+        for dy in (2, 1, 3, 0) for dlow in (1, 0) for dcore in (0, 1)
+        if (dy, dlow, dcore) != (0, 0, 0) and (dy, dlow) != (2, 1)
+    ]
     for target in targets:
         pl.semaphore_signal(barrier, inc=1, device_id=target, device_id_type=MESH)
+    halves = tuple(pl.ds(start, rows // 2) for start in (0, rows // 2))
     big = [
-        pltpu.make_async_copy(q_hbm, q_v, load_sem.at[8]),
-        pltpu.make_async_copy(c_hbm, c_v, load_sem.at[9]),
+        pltpu.make_async_copy(src.at[half], dst.at[half], load_sem.at[8 + 2 * i + j])
+        for i, half in enumerate(halves) for j, (src, dst) in enumerate(((q_hbm, q_v), (c_hbm, c_v)))
     ]
     for copy in big:
         copy.start()
@@ -137,7 +148,7 @@
     groups = tuple((local + a * own, local + b * own) for a, b in (NEAR, FAR))
     groups = ((0, groups[0][0]),) + groups
 
-    def score(group):
+    def score(group, first_block, last_block):
         lo, hi = groups[group]
 
         def step(block, carry):
@@ -176,11 +187,7 @@
                 d_st[a:b, at] = (soft * (grads - expected)).astype(BF16)
             return carry
 
-        lax.fori_loop(0, rows // BLK, step, 0, unroll=UNROLL)
-
-    for copy in big:
-        copy.wait()
-    score(0)
+        lax.fori_loop(first_block, last_block, step, 0, unroll=UNROLL)
 
     pl.semaphore_wait(barrier, len(targets))
     gathers = {}
@@ -196,23 +203,38 @@
         copy.start()
         gathers[there] = copy
 
-    for dz in (2, 1, 3):
+    half = rows // BLK // 2
+    for dz in (1, 3):
         pass_on(0, (dz, 0))
     for dx in (2, 1, 3):
         pass_on(0, (0, dx))
-    for dz in (1, 3, 2):
+    pl.semaphore_signal(token, inc=1, device_id=near_prompt(0, 1, 0), device_id_type=MESH)
+    for copy in big[:2]:
+        copy.wait()
+    score(0, 0, half)
+    for dz in (3, 1):
         block = OFFSETS.index((dz, 0))
         gathers[block].wait_recv()
+        if dz == 3:
+            pass_on(block, (1, 0))
         for dx in (2, 1, 3):
             pass_on(block, (0, dx))
+    for copy in big[2:]:
+        copy.wait()
+    score(0, half, 2 * half)
+    block = OFFSETS.index((2, 0))
+    gathers[block].wait_recv()
+    for dx in (2, 1, 3):
+        pass_on(block, (0, dx))
     for dx in (1, 3, 2):
         gathers[OFFSETS.index((0, dx))].wait_recv()
     place(*NEAR)
-    score(1)
+    score(1, 0, 2 * half)
     for p in range(*FAR):
         gathers[p].wait_recv()
     place(*FAR)
-    score(2)
+    score(2, 0, 2 * half)
+    pl.semaphore_wait(token, 1)
     for p in range(1, PEERS):
         gathers[p].wait_send()
     reward_sum = jnp.sum(gathered[:, :, lat:].astype(F32).reshape(PEERS * own, 2 * rope)[:, rope:]) / own
@@ -221,7 +243,8 @@
     def contract(stored, values, lo, hi):
         return jnp.dot(stored[...], values[:, lo:hi], preferred_element_type=F32)
 
-    reduces = []
+    along_x = []
+    order = [[local + own * OFFSETS.index((dz, dx)) for dz in range(LINE)] for dx in range(LINE)]
     for part, (lo, hi) in enumerate(PARTS):
         total = contract(d_st, q_v, lo, hi)
         if hi <= lat:
@@ -240,15 +263,42 @@
                 )
                 copy.start()
                 near.append(copy)
-        send_rows[:, :, lo:hi] = total[local:].astype(BF16).reshape(PEERS, own, hi - lo)
-        for p in range(PEERS - 1, 0, -1):
+        for dx in range(1, LINE):
+            for dz in range(LINE):
+                at = order[dx][dz]
+                send_x[dx, dz, :, lo:hi] = total[at : at + own].astype(BF16)
+        started = []
+        for dx in (2, 1, 3):
             copy = pltpu.make_async_remote_copy(
-                src_ref=send_rows.at[p, :, lo:hi], dst_ref=recv_rows.at[BACK[p], :, lo:hi],
-                send_sem=r_send.at[part, p], recv_sem=r_recv.at[part, BACK[p]],
-                device_id=same_prompt(p), device_id_type=MESH,
+                src_ref=send_x.at[dx, :, :, lo:hi], dst_ref=recv_x.at[dx, :, :, lo:hi],
+                send_sem=x_send.at[part, dx], recv_sem=x_recv.at[part, dx],
+                device_id=same_prompt(OFFSETS.index((0, dx))), device_id_type=MESH,
             )
             copy.start()
-            reduces.append(copy)
+            started.append(copy)
+        along_x.append(started)
+
+    along_z = []
+    for part, (lo, hi) in enumerate(PARTS):
+        for copy in along_x[part]:
+            copy.wait()
+        for dz in range(LINE):
+            at = order[0][dz]
+            total = acc[at : at + own, lo:hi]
+            for dx in range(1, LINE):
+                total = total + recv_x[dx, dz, :, lo:hi].astype(F32)
+            if dz == 0:
+                acc[at : at + own, lo:hi] = total
+            else:
+                send_z[dz, :, lo:hi] = total.astype(BF16)
+        for dz in (2, 1, 3):
+            copy = pltpu.make_async_remote_copy(
+                src_ref=send_z.at[dz, :, lo:hi], dst_ref=recv_z.at[dz, :, lo:hi],
+                send_sem=z_send.at[part, dz], recv_sem=z_recv.at[part, dz],
+                device_id=same_prompt(OFFSETS.index((dz, 0))), device_id_type=MESH,
+            )
+            copy.start()
+            along_z.append(copy)
 
     for copy in near:
         copy.wait()
@@ -268,11 +318,11 @@
 
     o_rl[...] = norm_backward(acc[:local, :lat], res_normed, res_inverse, gain)
     o_rr[...] = acc[:local, lat:].T
-    for copy in reduces:
+    for copy in along_z:
         copy.wait()
     total = acc[local : local + own, :]
-    for p in range(1, PEERS):
-        total = total + recv_rows[p].astype(F32)
+    for dz in range(1, LINE):
+        total = total + recv_z[dz].astype(F32)
     o_pl[...] = norm_backward(total[:, :lat], own_normed, own_inverse, gain)
     o_pr[...] = total[:, lat:]
 
@@ -320,17 +370,22 @@
             pltpu.SMEM((1, tokens), jnp.int32),
             pltpu.SMEM((1, 1), F32),
             vmem((count, wide), F32),
-            vmem((PEERS, own, wide), BF16),
-            vmem((PEERS, own, wide), BF16),
+            vmem((LINE, LINE, own, wide), BF16),
+            vmem((LINE, LINE, own, wide), BF16),
+            vmem((LINE, own, wide), BF16),
+            vmem((LINE, own, wide), BF16),
             vmem((1, lat), F32),
             vmem((PEERS, 1, lat), F32),
             vmem((1, lat), F32),
             vmem((PEERS, 1, lat), F32),
-            dma((10,)),
-            dma((PEERS,)),
-            dma((PEERS,)),
-            dma((len(PARTS), PEERS)),
-            dma((len(PARTS), PEERS)),
+            pltpu.SemaphoreType.REGULAR,
+            dma((12,)),
+            dma((PEERS,)),
+            dma((PEERS,)),
+            dma((len(PARTS), LINE)),
+            dma((len(PARTS), LINE)),
+            dma((len(PARTS), LINE)),
+            dma((len(PARTS), LINE)),
             dma((PEERS,)),
             dma((PEERS,)),
             dma((PEERS,)),

time: 52.9 us -> 47.7 us (0.902)
  Pallas kernels: 47.7 us -> 42.5 us
    pallas_call x1, Pallas kernels: 47.7 us -> 42.5 us  [per_device(): pl.pallas_call(kernel, out_shape=tuple((pltpu.VMEM(s, F32) for s in shape...]
where the time goes in v3:
time: 47.7 us; the launch traced here: 47.6 us
  Pallas kernels  42.5 us (89%)
  other arithmetic  3.1 us (6%)
  between operations  1.94 us (4%)
    pallas_call x1, Pallas kernels, per_device(): pl.pallas_call(kernel, out_shape=tuple((pltpu.VMEM(s, F32) for s in shape...  42.5 us

profile of v3, /device:TPU:1, one launch (start us, length us, event | category | flops | bytes accessed | tf_op | source)
XLA Modules:
  0.0 47.6 jit_solution(14359357188961439942)
XLA Ops:
  1.9 42.5 %grpo_backward.1 = (f32[16,512]{1,0:T(8,128)S(1)}, f32[16,64]{1,0:T(8,128)S(1)}, f32[80,512]{1,0:T(8,128)S(1)}, f32[64,80]{1,0:T(8,128)S(1)}, f32[1,512]{1,0:T(1,128)S(1)}) custom-call(bf16[16,512]{1,0:T(8,128)(2,1)} %bitcast.24, bf16[16,64]{1,0:T(8,128)(2,1)} %bitcast.26, bf16[80,512]{1,0:T(8,128)(2,1)} %bitcast.23, bf16[64,80]{1,0:T(8,128)(2,1)} %bitcast.25, ...), custom_call_target="tpu_custom_call" | custom-call | tf_op jit(solution)/shard_map/grpo_backward/pallas_call | solution.py:348
  44.5 0.6 %multiply_bitcast_fusion.2 = f32[1,16,512]{2,1,0:T(8,128)} fusion(f32[16,512]{1,0:T(8,128)S(1)} %get-tuple-element.10), kind=kLoop, calls=%fused_computation.2 | loop fusion | flops 8192 | bytes 65536 | tf_op jit(solution)/shard_map/broadcast_in_dim | solution.py:411
  45.1 0.6 %broadcast_multiply_fusion = f32[1,512]{1,0:T(1,128)} fusion(f32[1,512]{1,0:T(1,128)S(1)} %get-tuple-element.14), kind=kLoop, calls=%fused_computation.4 | loop fusion | flops 512 | bytes 4096 | tf_op jit(solution)/shard_map/mul | solution.py:410
  45.7 0.6 %multiply_bitcast_fusion.3 = f32[1,16,64]{2,1,0:T(8,128)} fusion(f32[16,64]{1,0:T(8,128)S(1)} %get-tuple-element.11), kind=kLoop, calls=%fused_computation.3 | loop fusion | flops 1024 | bytes 8192 | tf_op jit(solution)/shard_map/broadcast_in_dim | solution.py:411
  46.3 0.6 %multiply_bitcast_fusion.1 = f32[1,1,80,64]{2,3,1,0:T(8,128)} fusion(f32[64,80]{1,0:T(8,128)S(1)} %get-tuple-element.13), kind=kLoop, calls=%fused_computation.1 | loop fusion | flops 5120 | bytes 40960 | tf_op jit(solution)/shard_map/broadcast_in_dim | solution.py:411
  46.9 0.7 %multiply_bitcast_fusion = f32[1,1,80,512]{3,2,1,0:T(8,128)} fusion(f32[80,512]{1,0:T(8,128)S(1)} %get-tuple-element.12), kind=kLoop, calls=%fused_computation | loop fusion | flops 40960 | bytes 327680 | tf_op jit(solution)/shard_map/broadcast_in_dim | solution.py:411

commit v4 on v3

--- a/solution.py
+++ b/solution.py
@@ -69,8 +69,17 @@
         dz, dx = OFFSETS[position]
         return {"resp": shift(my_z, dz) * LINE + shift(my_x, dx)}
 
-    def same_response(step):
-        return {"prompt": lax.rem(prompt + step, PEERS)}
+    def same_plane(step):
+        return {
+            "prompt": shift(prompt // LINE, step // LINE) * LINE + lax.rem(prompt, LINE),
+            "resp": my_z * LINE + shift(my_x, step % LINE),
+        }
+
+    def same_column(step):
+        return {
+            "prompt": prompt // LINE * LINE + shift(lax.rem(prompt, LINE), step // LINE),
+            "resp": shift(my_z, step % LINE) * LINE + my_x,
+        }
 
     my_y, my_low, my_core = prompt // LINE, lax.rem(prompt, LINE) // 2, lax.rem(prompt, 2)
 
@@ -104,7 +113,7 @@
     ]
     for copy in big:
         copy.start()
-    for copy in small:
+    for copy in small[:3]:
         copy.wait()
 
     reward = jnp.full((own, rope), rew_s[0, 0], F32)
@@ -119,6 +128,27 @@
     gathered[0, :, :lat] = pl_v[...]
     gathered[0, :, lat:] = jnp.concatenate([pr_v[...].astype(F32), terms], axis=1).astype(BF16)
 
+    pl.semaphore_wait(barrier, len(targets))
+    gathers = {}
+
+    def pass_on(block, offset):
+        (dz, dx), (ez, ex) = OFFSETS[block], offset
+        there = OFFSETS.index(((dz - ez) % LINE, (dx - ex) % LINE))
+        copy = pltpu.make_async_remote_copy(
+            src_ref=gathered.at[block], dst_ref=gathered.at[there],
+            send_sem=g_send.at[there], recv_sem=g_recv.at[there],
+            device_id=same_prompt(OFFSETS.index(offset)), device_id_type=MESH,
+        )
+        copy.start()
+        gathers[there] = copy
+
+    for dz in (1, 3):
+        pass_on(0, (dz, 0))
+    for dx in (2, 1, 3):
+        pass_on(0, (0, dx))
+    for copy in small[3:]:
+        copy.wait()
+
     gain = gain_v[...]
     res_normed, res_inverse = normed_rows(rl_v[...])
     normed[:local, :] = res_normed
@@ -140,6 +170,7 @@
     own_normed, own_inverse = place(0, 1)
 
     heads = rows // local
+    half = rows // BLK // 2
     per_block = BLK // heads
     column = lax.broadcasted_iota(jnp.int32, (1, BLK), 1)
     key_at = lax.broadcasted_iota(jnp.int32, (local, BLK), 0)
@@ -189,26 +220,6 @@
 
         lax.fori_loop(first_block, last_block, step, 0, unroll=UNROLL)
 
-    pl.semaphore_wait(barrier, len(targets))
-    gathers = {}
-
-    def pass_on(block, offset):
-        (dz, dx), (ez, ex) = OFFSETS[block], offset
-        there = OFFSETS.index(((dz - ez) % LINE, (dx - ex) % LINE))
-        copy = pltpu.make_async_remote_copy(
-            src_ref=gathered.at[block], dst_ref=gathered.at[there],
-            send_sem=g_send.at[there], recv_sem=g_recv.at[there],
-            device_id=same_prompt(OFFSETS.index(offset)), device_id_type=MESH,
-        )
-        copy.start()
-        gathers[there] = copy
-
-    half = rows // BLK // 2
-    for dz in (1, 3):
-        pass_on(0, (dz, 0))
-    for dx in (2, 1, 3):
-        pass_on(0, (0, dx))
-    pl.semaphore_signal(token, inc=1, device_id=near_prompt(0, 1, 0), device_id_type=MESH)
     for copy in big[:2]:
         copy.wait()
     score(0, 0, half)
@@ -233,12 +244,14 @@
     for p in range(*FAR):
         gathers[p].wait_recv()
     place(*FAR)
+    for step in range(LINE, PEERS, LINE):
+        pl.semaphore_signal(token, inc=1, device_id=same_plane(step), device_id_type=MESH)
+        pl.semaphore_signal(token, inc=1, device_id=same_column(step), device_id_type=MESH)
     score(2, 0, 2 * half)
-    pl.semaphore_wait(token, 1)
     for p in range(1, PEERS):
         gathers[p].wait_send()
-    reward_sum = jnp.sum(gathered[:, :, lat:].astype(F32).reshape(PEERS * own, 2 * rope)[:, rope:]) / own
-    factor = reward_sum / PEERS - rew_s[0, 0]
+    reward_rows = jnp.sum(gathered[:, :, lat:].astype(F32).reshape(PEERS * own, 2 * rope)[:, rope:], axis=0, keepdims=True)
+    factor = jnp.sum(reward_rows, axis=1, keepdims=True) / (own * PEERS) - rew_s[0, 0]
 
     def contract(stored, values, lo, hi):
         return jnp.dot(stored[...], values[:, lo:hi], preferred_element_type=F32)
@@ -254,12 +267,13 @@
         if hi <= lat:
             gain_own[:, lo:hi] = jnp.sum(total * normed[:, lo:hi], axis=0, keepdims=True)
         if hi == lat:
+            pl.semaphore_wait(token, 2 * (LINE - 1))
             near = []
             for step in range(1, PEERS):
                 copy = pltpu.make_async_remote_copy(
-                    src_ref=gain_own, dst_ref=gain_a.at[BACK[step]],
-                    send_sem=a_send.at[step], recv_sem=a_recv.at[BACK[step]],
-                    device_id=same_prompt(step), device_id_type=MESH,
+                    src_ref=gain_own, dst_ref=gain_a.at[step],
+                    send_sem=a_send.at[step], recv_sem=a_recv.at[step],
+                    device_id=same_plane(step), device_id_type=MESH,
                 )
                 copy.start()
                 near.append(copy)
@@ -280,6 +294,22 @@
 
     along_z = []
     for part, (lo, hi) in enumerate(PARTS):
+        if part == len(PARTS) - 1:
+            for copy in near:
+                copy.wait()
+            total_gain = gain_own[...]
+            for step in range(1, PEERS):
+                total_gain = total_gain + gain_a[step]
+            gain_mid[...] = total_gain
+            far = []
+            for step in range(1, PEERS):
+                copy = pltpu.make_async_remote_copy(
+                    src_ref=gain_mid, dst_ref=gain_b.at[step],
+                    send_sem=b_send.at[step], recv_sem=b_recv.at[step],
+                    device_id=same_column(step), device_id_type=MESH,
+                )
+                copy.start()
+                far.append(copy)
         for copy in along_x[part]:
             copy.wait()
         for dz in range(LINE):
@@ -300,22 +330,6 @@
             copy.start()
             along_z.append(copy)
 
-    for copy in near:
-        copy.wait()
-    total_gain = gain_own[...]
-    for step in range(1, PEERS):
-        total_gain = total_gain + gain_a[step]
-    gain_mid[...] = total_gain
-    far = []
-    for step in range(1, PEERS):
-        copy = pltpu.make_async_remote_copy(
-            src_ref=gain_mid, dst_ref=gain_b.at[step],
-            send_sem=b_send.at[step], recv_sem=b_recv.at[step],
-            device_id=same_response(step), device_id_type=MESH,
-        )
-        copy.start()
-        far.append(copy)
-
     o_rl[...] = norm_backward(acc[:local, :lat], res_normed, res_inverse, gain)
     o_rr[...] = acc[:local, lat:].T
     for copy in along_z:
@@ -348,7 +362,7 @@
     out = pl.pallas_call(
         kernel,
         out_shape=tuple(pltpu.VMEM(s, F32) for s in shapes),
-        in_specs=[pl.BlockSpec(memory_space=pl.ANY)] * 10,
+        in_specs=[pl.BlockSpec(memory_space=pltpu.HBM)] * 10,
         out_specs=[pl.BlockSpec(memory_space=pltpu.VMEM)] * 5,
         scratch_shapes=[
             vmem((rows, wide), BF16),

time: 47.7 us -> 47.2 us (0.990)
  Pallas kernels: 42.5 us -> 42 us
    pallas_call x1, Pallas kernels: 42.5 us -> 42 us  [per_device(): pl.pallas_call(kernel, out_shape=tuple((pltpu.VMEM(s, F32) for s in shape...]
where the time goes in v4:
time: 47.2 us; the launch traced here: 47.1 us
  Pallas kernels  42 us (89%)
  other arithmetic  3.1 us (7%)
  between operations  1.94 us (4%)
    pallas_call x1, Pallas kernels, per_device(): pl.pallas_call(kernel, out_shape=tuple((pltpu.VMEM(s, F32) for s in shape...  42 us

profile of v4, /device:TPU:1, one launch (start us, length us, event | category | flops | bytes accessed | tf_op | source)
XLA Modules:
  0.0 47.1 jit_solution(14909794315323434590)
XLA Ops:
  1.9 42.0 %grpo_backward.1 = (f32[16,512]{1,0:T(8,128)S(1)}, f32[16,64]{1,0:T(8,128)S(1)}, f32[80,512]{1,0:T(8,128)S(1)}, f32[64,80]{1,0:T(8,128)S(1)}, f32[1,512]{1,0:T(1,128)S(1)}) custom-call(bf16[16,512]{1,0:T(8,128)(2,1)} %bitcast.24, bf16[16,64]{1,0:T(8,128)(2,1)} %bitcast.26, bf16[80,512]{1,0:T(8,128)(2,1)} %bitcast.23, bf16[64,80]{1,0:T(8,128)(2,1)} %bitcast.25, ...), custom_call_target="tpu_custom_call" | custom-call | tf_op jit(solution)/shard_map/grpo_backward/pallas_call | solution.py:362
  44.0 0.6 %multiply_bitcast_fusion.2 = f32[1,16,512]{2,1,0:T(8,128)} fusion(f32[16,512]{1,0:T(8,128)S(1)} %get-tuple-element.10), kind=kLoop, calls=%fused_computation.2 | loop fusion | flops 8192 | bytes 65536 | tf_op jit(solution)/shard_map/broadcast_in_dim | solution.py:425
  44.6 0.6 %broadcast_multiply_fusion = f32[1,512]{1,0:T(1,128)} fusion(f32[1,512]{1,0:T(1,128)S(1)} %get-tuple-element.14), kind=kLoop, calls=%fused_computation.4 | loop fusion | flops 512 | bytes 4096 | tf_op jit(solution)/shard_map/mul | solution.py:424
  45.2 0.6 %multiply_bitcast_fusion.3 = f32[1,16,64]{2,1,0:T(8,128)} fusion(f32[16,64]{1,0:T(8,128)S(1)} %get-tuple-element.11), kind=kLoop, calls=%fused_computation.3 | loop fusion | flops 1024 | bytes 8192 | tf_op jit(solution)/shard_map/broadcast_in_dim | solution.py:425
  45.8 0.6 %multiply_bitcast_fusion.1 = f32[1,1,80,64]{2,3,1,0:T(8,128)} fusion(f32[64,80]{1,0:T(8,128)S(1)} %get-tuple-element.13), kind=kLoop, calls=%fused_computation.1 | loop fusion | flops 5120 | bytes 40960 | tf_op jit(solution)/shard_map/broadcast_in_dim | solution.py:425
  46.4 0.7 %multiply_bitcast_fusion = f32[1,1,80,512]{3,2,1,0:T(8,128)} fusion(f32[80,512]{1,0:T(8,128)S(1)} %get-tuple-element.12), kind=kLoop, calls=%fused_computation | loop fusion | flops 40960 | bytes 327680 | tf_op jit(solution)/shard_map/broadcast_in_dim | solution.py:425

commit v5 on v4

--- a/solution.py
+++ b/solution.py
@@ -41,6 +41,7 @@
 )
 BACK = [OFFSETS.index(((LINE - dz) % LINE, (LINE - dx) % LINE)) for dz, dx in OFFSETS]
 NEAR, FAR = (1, 7), (7, 16)
+LATE = 13
 PARTS = ((0, 256), (256, 512), (512, 576))
 
 
@@ -102,7 +103,7 @@
     targets += [
         near_prompt(dy, dlow, dcore)
         for dy in (2, 1, 3, 0) for dlow in (1, 0) for dcore in (0, 1)
-        if (dy, dlow, dcore) != (0, 0, 0) and (dy, dlow) != (2, 1)
+        if (dy > 0) != (dlow + dcore > 0)
     ]
     for target in targets:
         pl.semaphore_signal(barrier, inc=1, device_id=target, device_id_type=MESH)
@@ -241,9 +242,10 @@
         gathers[OFFSETS.index((0, dx))].wait_recv()
     place(*NEAR)
     score(1, 0, 2 * half)
-    for p in range(*FAR):
-        gathers[p].wait_recv()
-    place(*FAR)
+    for first, last in ((FAR[0], LATE), (LATE, FAR[1])):
+        for p in range(first, last):
+            gathers[p].wait_recv()
+        place(first, last)
     for step in range(LINE, PEERS, LINE):
         pl.semaphore_signal(token, inc=1, device_id=same_plane(step), device_id_type=MESH)
         pl.semaphore_signal(token, inc=1, device_id=same_column(step), device_id_type=MESH)

time: 47.2 us -> 47.3 us (level)
  no operation moved by 1% of the time
where the time goes in v5:
time: 47.3 us; the launch traced here: 47.2 us
  Pallas kernels  42.1 us (89%)
  other arithmetic  3.1 us (7%)
  between operations  1.94 us (4%)
    pallas_call x1, Pallas kernels, per_device(): pl.pallas_call(kernel, out_shape=tuple((pltpu.VMEM(s, F32) for s in shape...  42.1 us

profile of v5, /device:TPU:1, one launch (start us, length us, event | category | flops | bytes accessed | tf_op | source)
XLA Modules:
  0.0 47.2 jit_solution(66346166872333074)
XLA Ops:
  1.9 42.1 %grpo_backward.1 = (f32[16,512]{1,0:T(8,128)S(1)}, f32[16,64]{1,0:T(8,128)S(1)}, f32[80,512]{1,0:T(8,128)S(1)}, f32[64,80]{1,0:T(8,128)S(1)}, f32[1,512]{1,0:T(1,128)S(1)}) custom-call(bf16[16,512]{1,0:T(8,128)(2,1)} %bitcast.24, bf16[16,64]{1,0:T(8,128)(2,1)} %bitcast.26, bf16[80,512]{1,0:T(8,128)(2,1)} %bitcast.23, bf16[64,80]{1,0:T(8,128)(2,1)} %bitcast.25, ...), custom_call_target="tpu_custom_call" | custom-call | tf_op jit(solution)/shard_map/grpo_backward/pallas_call | solution.py:364
  44.1 0.6 %multiply_bitcast_fusion.2 = f32[1,16,512]{2,1,0:T(8,128)} fusion(f32[16,512]{1,0:T(8,128)S(1)} %get-tuple-element.10), kind=kLoop, calls=%fused_computation.2 | loop fusion | flops 8192 | bytes 65536 | tf_op jit(solution)/shard_map/broadcast_in_dim | solution.py:427
  44.7 0.6 %broadcast_multiply_fusion = f32[1,512]{1,0:T(1,128)} fusion(f32[1,512]{1,0:T(1,128)S(1)} %get-tuple-element.14), kind=kLoop, calls=%fused_computation.4 | loop fusion | flops 512 | bytes 4096 | tf_op jit(solution)/shard_map/mul | solution.py:426
  45.3 0.6 %multiply_bitcast_fusion.3 = f32[1,16,64]{2,1,0:T(8,128)} fusion(f32[16,64]{1,0:T(8,128)S(1)} %get-tuple-element.11), kind=kLoop, calls=%fused_computation.3 | loop fusion | flops 1024 | bytes 8192 | tf_op jit(solution)/shard_map/broadcast_in_dim | solution.py:427
  45.9 0.6 %multiply_bitcast_fusion.1 = f32[1,1,80,64]{2,3,1,0:T(8,128)} fusion(f32[64,80]{1,0:T(8,128)S(1)} %get-tuple-element.13), kind=kLoop, calls=%fused_computation.1 | loop fusion | flops 5120 | bytes 40960 | tf_op jit(solution)/shard_map/broadcast_in_dim | solution.py:427
  46.5 0.7 %multiply_bitcast_fusion = f32[1,1,80,512]{3,2,1,0:T(8,128)} fusion(f32[80,512]{1,0:T(8,128)S(1)} %get-tuple-element.12), kind=kLoop, calls=%fused_computation | loop fusion | flops 40960 | bytes 327680 | tf_op jit(solution)/shard_map/broadcast_in_dim | solution.py:427
